TPU v7x, 32 devices: a whole 2x2x4 slice. The times are simulated.
32 devices in a mesh: row: 8 (over z, x), col: 4 (over y, core).
Axes of the slice: x: 2, y: 2, z: 4, core: 2. Of those that a mesh axis runs over, the one named last changes fastest.
Arguments:
- x_rhs: bfloat16 [16, 1024, 1024], P('col', 'row'), may hold values from -6 to 6
- panel_u: bfloat16 [16, 1024, 256], P('row', 'col'), may hold values from -0.1875 to 0.1875
- panel_v: bfloat16 [16, 1024, 256], P('row', 'col'), may hold values from -0.1875 to 0.1875
- panel_rank: int32 [16], replicated, may hold values from 32 to 256, as said below
- tile_p: bfloat16 [16, 16, 1024, 256], P('row', 'col'), may hold values from -0.09375 to 0.09375
- tile_q: bfloat16 [16, 16, 1024, 256], P('row', 'col'), may hold values from -0.1875 to 0.1875
- tile_rank: int32 [16, 16], P('row', 'col'), may hold values from 32 to 256, as said below
Outputs:
- kriged: bfloat16 [16, 1024, 1024], P('row', None, 'col')
Inputs may be any that keep to these rules, and one draw needn't show every extreme that they name: `panel_rank`: each panel tile's rank; the columns at or beyond it carry no part of the tile. `tile_rank`: each trailing tile's rank; the columns at or beyond it carry no part of the tile.
All inputs are finite; a program needn't handle non-finite values.
Results may differ from a plain program's by a relative error of at most 0.018.
Values may be sent and summed in bfloat16 or wider, within the bound.
A program may use at most 64 MiB of HBM per device.

v0:
```python
import functools

import jax
import jax.numpy as jnp
from jax import lax
from jax.experimental import pallas as pl
from jax.experimental.pallas import tpu as pltpu
from jax.sharding import PartitionSpec as P

BF16 = jnp.bfloat16
F32 = jnp.float32
MESH = pl.DeviceIdType.MESH
UP, DOWN, ACROSS = 0, 1, 2


def plain(x_rhs, panel_u, panel_v, panel_rank, tile_p, tile_q, tile_rank):
    exact = lax.Precision.HIGHEST
    row_at = lax.axis_index("row")
    col_at = lax.axis_index("col")
    t_rows = tile_p.shape[0]
    t_cols = tile_p.shape[1]
    rank_cap = tile_p.shape[3]
    gathered = lax.all_gather(x_rhs, "row", axis=1, tiled=True)
    full_u, full_v = (
        lax.all_gather(panel_u, "col", axis=1, tiled=True),
        lax.all_gather(panel_v, "col", axis=1, tiled=True),
    )
    tile_slot = lax.broadcasted_iota(jnp.int32, (1, 1, rank_cap, 1), 2)
    tile_proj = jnp.einsum("ijbr,jbn->ijrn", tile_q, gathered, preferred_element_type=jnp.float32)
    tile_proj = jnp.where(tile_slot < tile_rank[:, :, None, None], tile_proj, 0.0).astype(
        jnp.bfloat16
    )
    base_sum = jnp.einsum("ijbr,ijrn->ibn", tile_p, tile_proj, preferred_element_type=jnp.float32)
    rank_slot = lax.broadcasted_iota(jnp.int32, (1, rank_cap, 1), 1)
    row_rank = lax.dynamic_slice_in_dim(panel_rank, row_at * t_rows, t_rows)
    row_keep = rank_slot < row_rank[:, None, None]
    u_wide = full_u.astype(jnp.float32)
    tile_ids = row_at * t_rows + jnp.arange(t_rows, dtype=jnp.int32)
    inside = tile_ids // t_cols == col_at
    where_rhs = jnp.clip(tile_ids - col_at * t_cols, 0, t_cols - 1)
    picked = jnp.take(gathered, where_rhs, axis=0)
    keep = jnp.logical_and(inside[:, None, None], row_keep)
    panel_proj = jnp.einsum("jbr,jbn->jrn", full_u, picked, preferred_element_type=jnp.float32)
    panel_proj = jnp.where(keep, panel_proj, 0.0).astype(jnp.bfloat16)
    sweep_part = jnp.einsum("jbr,jrn->bn", full_v, panel_proj, preferred_element_type=jnp.float32)
    sweep_share = lax.psum_scatter(
        sweep_part.astype(jnp.bfloat16), "col", scatter_dimension=1, tiled=True
    )
    sweep = lax.psum(sweep_share, "row").astype(jnp.float32)
    back_proj = jnp.einsum("ibr,bn->irn", full_v.astype(jnp.float32), sweep, precision=exact)
    back_proj = jnp.where(row_keep, back_proj, 0.0)
    late_term = jnp.einsum("ibr,irn->ibn", u_wide, back_proj, precision=exact)
    summed = lax.psum_scatter(
        base_sum.astype(jnp.bfloat16), "col", scatter_dimension=2, tiled=True
    ).astype(jnp.float32)
    return (summed - late_term).astype(jnp.bfloat16)


def dot(a, b):
    return jnp.dot(a, b, preferred_element_type=F32)


def kernel(
    n_row, n_col,
    tile_rank, panel_rank, x_in, u_in, v_in, p_in, q_in,
    out,
    xg, pv, qv, qt, ug, vg, ut, vt, acc, sweep_acc, sbuf, rbuf, swb, swr, swg,
    x_send, x_recv, h_send, h_recv, uv_send, uv_recv, b_send, b_recv, sw_send, sw_recv, g_send, g_recv, local,
):
    t_rows, t_cols, order, rank_cap = pv.shape
    x_rows = xg.shape[3]
    width = xg.shape[4]
    u_rows = ug.shape[2]
    subs = swr.shape[0]
    steps = n_col * subs
    away = steps - subs
    ahead = 2
    half = t_cols // 2
    line = n_row // 2
    row = lax.axis_index("row")
    col = lax.axis_index("col")
    z, x = row // 2, row % 2
    mate = row + 1 - 2 * x
    odd = z % 2 == 1
    twin = row + 2 - 4 * (z % 2)
    inside = (row * t_rows) // t_cols == col
    first = lax.rem(row * t_rows, t_cols)

    def owner(s):
        return lax.rem(col + 1 + s // subs, n_col)

    def x_local(s):
        at = pl.multiple_of((owner(s) * subs + lax.rem(s, subs)) * width, width)
        return pltpu.make_async_copy(x_in.at[:, :, pl.ds(at, width)], xg.at[s, row], local.at[s])

    q_local = pltpu.make_async_copy(q_in, qv, local.at[steps])
    p_local = pltpu.make_async_copy(p_in, pv, local.at[steps + 1])
    u_local = pltpu.make_async_copy(u_in, ug.at[col], local.at[steps + 2])
    v_local = pltpu.make_async_copy(v_in, vg.at[col], local.at[steps + 3])
    x_local(0).start()
    u_local.start()
    v_local.start()
    for s in range(1, steps):
        x_local(s).start()
    q_local.start()
    p_local.start()

    barrier = pltpu.get_barrier_semaphore()

    @pl.loop(0, n_row * n_col)
    def _(k):
        @pl.when(k != row * n_col + col)
        def _():
            pl.semaphore_signal(
                barrier, inc=1, device_id=(k // n_col, lax.rem(k, n_col)), device_id_type=MESH
            )

    pl.semaphore_wait(barrier, n_row * n_col - 1)

    def x_copy(s, k, way):
        target = {UP: row + 2, DOWN: row - 2, ACROSS: mate}[way]
        return pltpu.make_async_remote_copy(
            src_ref=xg.at[s, k], dst_ref=xg.at[s, k],
            send_sem=x_send.at[s, k, way], recv_sem=x_recv.at[s, k],
            device_id=(target, col), device_id_type=MESH,
        )

    def low_copy(s, k):
        return pltpu.make_async_remote_copy(
            src_ref=xg.at[s, k, :half], dst_ref=xg.at[s, k, :half],
            send_sem=x_send.at[s, k, ACROSS], recv_sem=x_recv.at[s, k],
            device_id=(mate, col), device_id_type=MESH,
        )

    def high_copy(s, k):
        return pltpu.make_async_remote_copy(
            src_ref=xg.at[s, k, half:], dst_ref=xg.at[s, k, half:],
            send_sem=h_send.at[s], recv_sem=h_recv.at[s],
            device_id=(twin, col), device_id_type=MESH,
        )

    def across(s, k, is_twin):
        @pl.when(is_twin)
        def _():
            low_copy(s, k).start()

        @pl.when(jnp.logical_not(is_twin))
        def _():
            x_copy(s, k, ACROSS).start()

    def own_sends(s):
        x_local(s).wait()
        x_copy(s, row, ACROSS).start()

        @pl.when(z + 1 < line)
        def _():
            x_copy(s, row, UP).start()

        @pl.when(z > 0)
        def _():
            x_copy(s, row, DOWN).start()

    def forward(s, d):
        @pl.when(z - d >= 0)
        def _():
            k = row - 2 * d
            x_copy(s, k, ACROSS).wait_recv()
            across(s, k, odd) if d == 1 else x_copy(s, k, ACROSS).start()

            @pl.when(z + 1 < line)
            def _():
                x_copy(s, k, UP).start()

        @pl.when(z + d < line)
        def _():
            k = row + 2 * d
            x_copy(s, k, ACROSS).wait_recv()
            across(s, k, jnp.logical_not(odd)) if d == 1 else x_copy(s, k, ACROSS).start()

            @pl.when(z > 0)
            def _():
                x_copy(s, k, DOWN).start()

    def uv_copy(which, d, slot):
        ref = (ug, vg)[which]
        return pltpu.make_async_remote_copy(
            src_ref=ref.at[slot], dst_ref=ref.at[slot],
            send_sem=uv_send.at[which, d], recv_sem=uv_recv.at[which, d],
            device_id=(row, lax.rem(col + d, n_col)), device_id_type=MESH,
        )

    own_sends(0)
    u_local.wait()
    v_local.wait()
    for d in range(1, n_col):
        uv_copy(0, d, col).start()
        uv_copy(1, d, col).start()
    for s in range(1, ahead):
        own_sends(s)

    q_local.wait()

    @pl.loop(0, t_rows * t_cols)
    def _(k):
        i, j = k // t_cols, lax.rem(k, t_cols)
        keep = lax.broadcasted_iota(jnp.int32, (rank_cap, u_rows), 0) < tile_rank[i, j]
        for b in range(order // u_rows):
            at = pl.ds(b * u_rows, u_rows)
            qt[i, j, :, at] = jnp.where(keep, qv[i, j, at, :].T, jnp.zeros((), BF16))

    p_local.wait()
    for d in range(1, n_col):
        slot = lax.rem(col + n_col - d, n_col)
        uv_copy(0, d, slot).wait_recv()
        uv_copy(1, d, slot).wait_recv()

    @pl.loop(0, t_rows)
    def _(i):
        keep = (
            lax.broadcasted_iota(jnp.int32, (rank_cap, u_rows), 0) < panel_rank[row * t_rows + i]
        )
        for b in range(n_col):
            at = pl.ds(b * u_rows, u_rows)
            ut[i, :, at] = jnp.where(keep, ug[b, i].T, jnp.zeros((), BF16))
            vt[i, :, at] = jnp.where(keep, vg[b, i].T, jnp.zeros((), BF16))

    def b_copy(s):
        return pltpu.make_async_remote_copy(
            src_ref=sbuf.at[s], dst_ref=rbuf.at[s],
            send_sem=b_send.at[s], recv_sem=b_recv.at[s],
            device_id=(row, owner(s)), device_id_type=MESH,
        )

    def sw_copy(s, k):
        return pltpu.make_async_remote_copy(
            src_ref=swb.at[s, k], dst_ref=swr.at[lax.rem(s, subs), row],
            send_sem=sw_send.at[s, k], recv_sem=sw_recv.at[lax.rem(s, subs), row],
            device_id=(k, owner(s)), device_id_type=MESH,
        )

    def compute(s):
        low_copy(s, twin + 1 - 2 * x).wait_recv()
        high_copy(s, twin + 1 - 2 * x).wait_recv()
        for e in range(1, line // 2):
            pair = lax.rem(z // 2 + e, line // 2)
            for b in range(2):
                x_copy(s, 2 * (2 * pair + b) + 1 - x, ACROSS).wait_recv()

        @pl.when(inside)
        def _():
            for i in range(t_rows):
                block = xg[s, :, first + i].reshape(order, width)
                proj = dot(ut[i], block).astype(BF16)
                term = dot(vg[:, i].reshape(order, rank_cap), proj)
                if i == 0:
                    sweep_acc[...] = term
                else:
                    sweep_acc[...] += term
            swb[s] = sweep_acc[...].astype(BF16).reshape(n_row, x_rows, width)

            @pl.loop(0, n_row)
            def _(k):
                mine = jnp.logical_and(k == row, s >= away)

                @pl.when(mine)
                def _():
                    swr[s - away, row] = swb[s, row]

                @pl.when(jnp.logical_not(mine))
                def _():
                    sw_copy(s, k).start()

        @pl.loop(0, t_rows)
        def _(i):
            total = None
            for j in range(t_cols):
                proj = dot(qt[i, j], xg[s, :, j].reshape(order, width)).astype(BF16)
                term = dot(pv[i, j], proj)
                total = term if total is None else total + term

            @pl.when(s < away)
            def _():
                sbuf[s, i] = total.astype(BF16)

            @pl.when(s >= away)
            def _():
                acc[lax.rem(s, subs), i] = total

        @pl.when(s < away)
        def _():
            b_copy(s).start()

    def reduce_sweep(h):
        for k in range(n_row):
            @pl.when(jnp.logical_not(jnp.logical_and(inside, k == row)))
            def _():
                pltpu.make_async_remote_copy(
                    src_ref=swr.at[h, k], dst_ref=swr.at[h, k],
                    send_sem=sw_send.at[h, k], recv_sem=sw_recv.at[h, k],
                    device_id=(row, col), device_id_type=MESH,
                ).wait_recv()

        total = swr[h, 0].astype(F32)
        for k in range(1, n_row):
            total = total + swr[h, k].astype(F32)
        swg[h, row] = total.astype(BF16)
        for d in range(1, n_row):
            g_copy(h, d, row).start()

    def g_copy(h, d, slot):
        return pltpu.make_async_remote_copy(
            src_ref=swg.at[h, slot], dst_ref=swg.at[h, slot],
            send_sem=g_send.at[h, d], recv_sem=g_recv.at[h, d],
            device_id=(lax.rem(row + d, n_row), col), device_id_type=MESH,
        )

    def add_received(h):
        for g in range(n_col - 1):
            b_copy(g * subs + h).wait_recv()

        @pl.loop(0, t_rows)
        def _(i):
            total = acc[h, i]
            for g in range(n_col - 1):
                total = total + rbuf[g * subs + h, i].astype(F32)
            acc[h, i] = total

    def finish(h):
        for d in range(1, n_row):
            g_copy(h, d, lax.rem(row + n_row - d, n_row)).wait_recv()

        @pl.loop(0, t_rows)
        def _(i):
            back = dot(vt[i], swg[h].reshape(order, width)).astype(BF16)
            late = dot(ug[:, i].reshape(order, rank_cap), back)
            out[i, :, h * width : (h + 1) * width] = (acc[h, i] - late).astype(BF16)

    @pl.loop(0, steps + 1)
    def _(s):
        @pl.when(s < steps)
        def _():
            forward(s, 1)
            x_copy(s, mate, ACROSS).wait_recv()
            high_copy(s, mate).start()

        @pl.when(s + ahead < steps)
        def _():
            own_sends(s + ahead)

        @pl.when(s == steps)
        def _():
            for h in range(subs - 1):
                reduce_sweep(h)

        @pl.when(s > 0)
        def _():
            compute(s - 1)

        @pl.when(s < steps)
        def _():
            for d in range(2, line):
                forward(s, d)

    reduce_sweep(subs - 1)
    for h in range(subs):
        add_received(h)
    for h in range(subs):
        finish(h)

    @pl.loop(0, steps)
    def _(s):
        for m in range(line):
            k = 2 * m + x
            @pl.when(k == twin)
            def _():
                low_copy(s, k).wait_send()

            @pl.when(k != twin)
            def _():
                x_copy(s, k, ACROSS).wait_send()

            @pl.when(jnp.logical_and(m <= z, z + 1 < line))
            def _():
                x_copy(s, k, UP).wait_send()

            @pl.when(jnp.logical_and(m >= z, z > 0))
            def _():
                x_copy(s, k, DOWN).wait_send()

        high_copy(s, mate).wait_send()

        @pl.when(s < away)
        def _():
            b_copy(s).wait_send()

        @pl.when(inside)
        def _():
            @pl.loop(0, n_row)
            def _(k):
                @pl.when(jnp.logical_not(jnp.logical_and(k == row, s >= away)))
                def _():
                    sw_copy(s, k).wait_send()

    for d in range(1, n_col):
        uv_copy(0, d, col).wait_send()
        uv_copy(1, d, col).wait_send()
    for h in range(subs):
        for d in range(1, n_row):
            g_copy(h, d, row).wait_send()


def shards(n_row, n_col, x_rhs, panel_u, panel_v, panel_rank, tile_p, tile_q, tile_rank):
    t_rows, t_cols, order, rank_cap = tile_p.shape
    x_rows, n_rhs = x_rhs.shape[1:]
    u_rows = panel_u.shape[1]
    width = n_rhs // n_col
    subs = 1
    part = width // subs
    steps = n_col * subs
    away = steps - subs
    fits = (
        n_rhs % n_col == 0
        and width % (128 * subs) == 0
        and x_rows % 16 == 0
        and u_rows % 128 == 0
        and n_row % 4 == 0
        and n_col > 1
        and t_cols % t_rows == 0
        and t_cols % 2 == 0
    )
    if not fits:
        return plain(x_rhs, panel_u, panel_v, panel_rank, tile_p, tile_q, tile_rank)
    dma = pltpu.SemaphoreType.DMA
    flops = 4 * order * rank_cap * n_rhs * t_rows * (t_cols + 1)
    return pl.pallas_call(
        functools.partial(kernel, n_row, n_col),
        out_shape=jax.ShapeDtypeStruct((t_rows, order, width), BF16),
        in_specs=[pl.BlockSpec(memory_space=pltpu.SMEM)] * 2
        + [pl.BlockSpec(memory_space=pl.ANY)] * 5,
        out_specs=pl.BlockSpec(memory_space=pltpu.VMEM),
        scratch_shapes=[
            pltpu.VMEM((steps, n_row, t_cols, x_rows, part), BF16),
            pltpu.VMEM(tile_p.shape, BF16),
            pltpu.VMEM(tile_q.shape, BF16),
            pltpu.VMEM((t_rows, t_cols, rank_cap, order), BF16),
            pltpu.VMEM((n_col, t_rows, u_rows, rank_cap), BF16),
            pltpu.VMEM((n_col, t_rows, u_rows, rank_cap), BF16),
            pltpu.VMEM((t_rows, rank_cap, order), BF16),
            pltpu.VMEM((t_rows, rank_cap, order), BF16),
            pltpu.VMEM((subs, t_rows, order, part), F32),
            pltpu.VMEM((order, part), F32),
            pltpu.VMEM((away, t_rows, order, part), BF16),
            pltpu.VMEM((away, t_rows, order, part), BF16),
            pltpu.VMEM((steps, n_row, x_rows, part), BF16),
            pltpu.VMEM((subs, n_row, x_rows, part), BF16),
            pltpu.VMEM((subs, n_row, x_rows, part), BF16),
            dma((steps, n_row, 3)),
            dma((steps, n_row)),
            dma((steps,)),
            dma((steps,)),
            dma((2, n_col)),
            dma((2, n_col)),
            dma((away,)),
            dma((away,)),
            dma((steps, n_row)),
            dma((subs, n_row)),
            dma((subs, n_row)),
            dma((subs, n_row)),
            dma((steps + 4,)),
        ],
        compiler_params=pltpu.CompilerParams(
            collective_id=0, has_side_effects=True, vmem_limit_bytes=56 * 2**20
        ),
        cost_estimate=pl.CostEstimate(flops=flops, bytes_accessed=20 * 2**20, transcendentals=0),
    )(tile_rank, panel_rank, x_rhs, panel_u, panel_v, tile_p, tile_q)


def solution(mesh):
    return jax.shard_map(
        functools.partial(shards, mesh.shape["row"], mesh.shape["col"]),
        mesh=mesh,
        in_specs=(
            P("col", "row", None),
            P("row", "col", None),
            P("row", "col", None),
            P(),
            P("row", "col", None, None),
            P("row", "col", None, None),
            P("row", "col"),
        ),
        out_specs=P("row", None, "col"),
        check_vma=False,
    )
```

profile of v0, /device:TPU:29, one launch (start us, length us, event | category | flops | bytes accessed | tf_op | source)
XLA Modules:
  0.0 130.7 jit_solution(907675689575763785)
XLA Ops:
  0.0 128.4 %shard_map.73 = bf16[2,1024,256]{2,1,0:T(8,128)(2,1)} custom-call(s32[2,4]{1,0:T(2,128)} %tile_rank.1, s32[16]{0:T(128)} %panel_rank.1, bf16[4,128,1024]{2,1,0:T(8,128)(2,1)} %x_in.1, bf16[2,256,256]{2,1,0:T(8,128)(2,1)} %u_in.1, bf16[2,256,256]{2,1,0:T(8,128)(2,1)} %v_in.1, bf16[2,4,1024,256]{3,2,1,0:T(8,128)(2,1)} %p_in.1, bf16[2,4,1024,256]{3,2,1,0:T(8,128)(2,1)} %q_in.1), custom_call_target="tpu_custom_call" | custom-call | flops 10737418240 | bytes 20971520 | tf_op jit(solution)/shard_map/pallas_call | solution.py:435
  128.4 2.3 %copy.9 = bf16[2,1024,256]{2,1,0:T(8,128)(2,1)} copy(bf16[2,1024,256]{2,1,0:T(8,128)(2,1)} %shard_map.73) | data formatting | bytes 2097152
where the time goes:
time: 131 us
  Pallas kernels  128 us (98%)
  local copies, waits for them, and re-layouts  2.26 us (2%)
    pallas_call x1, Pallas kernels, shards(): pl.pallas_call(functools.partial(kernel, n_row, n_col), out_shape=jax.Sha...  128 us

commit v1 on v0

--- a/solution.py
+++ b/solution.py
@@ -87,7 +87,9 @@
     first = lax.rem(row * t_rows, t_cols)
 
     def owner(s):
-        return lax.rem(col + 1 + s // subs, n_col)
+        flip = n_col - 1 - s // subs
+        bits = [1 << b for b in range(n_col.bit_length() - 1)]
+        return sum(lax.rem(col // b + flip // b, 2) * b for b in bits)
 
     def x_local(s):
         at = pl.multiple_of((owner(s) * subs + lax.rem(s, subs)) * width, width)
@@ -352,14 +354,14 @@
             for h in range(subs - 1):
                 reduce_sweep(h)
 
-        @pl.when(s > 0)
-        def _():
-            compute(s - 1)
-
         @pl.when(s < steps)
         def _():
             for d in range(2, line):
                 forward(s, d)
+
+        @pl.when(s > 0)
+        def _():
+            compute(s - 1)
 
     reduce_sweep(subs - 1)
     for h in range(subs):
@@ -425,6 +427,7 @@
         and u_rows % 128 == 0
         and n_row % 4 == 0
         and n_col > 1
+        and n_col & (n_col - 1) == 0
         and t_cols % t_rows == 0
         and t_cols % 2 == 0
     )

time: 131 us -> 126 us (0.962); the launches traced: 131 us -> 124 us
  Pallas kernels: 128 us -> 121 us
    pallas_call x1, Pallas kernels: 128 us -> 121 us  [shards(): pl.pallas_call(functools.partial(kernel, n_row, n_col), out_shape=jax.Sha...]
where the time goes in v1:
time: 126 us; the launch traced here: 124 us
  Pallas kernels  121 us (96%)
  local copies, waits for them, and re-layouts  2.26 us (2%)
    pallas_call x1, Pallas kernels, shards(): pl.pallas_call(functools.partial(kernel, n_row, n_col), out_shape=jax.Sha...  121 us

profile of v1, /device:TPU:29, one launch (start us, length us, event | category | flops | bytes accessed | tf_op | source)
XLA Modules:
  0.0 123.6 jit_solution(15583152318944097797)
XLA Ops:
  0.0 121.3 %shard_map.73 = bf16[2,1024,256]{2,1,0:T(8,128)(2,1)} custom-call(s32[2,4]{1,0:T(2,128)} %tile_rank.1, s32[16]{0:T(128)} %panel_rank.1, bf16[4,128,1024]{2,1,0:T(8,128)(2,1)} %x_in.1, bf16[2,256,256]{2,1,0:T(8,128)(2,1)} %u_in.1, bf16[2,256,256]{2,1,0:T(8,128)(2,1)} %v_in.1, bf16[2,4,1024,256]{3,2,1,0:T(8,128)(2,1)} %p_in.1, bf16[2,4,1024,256]{3,2,1,0:T(8,128)(2,1)} %q_in.1), custom_call_target="tpu_custom_call" | custom-call | flops 10737418240 | bytes 20971520 | tf_op jit(solution)/shard_map/pallas_call | solution.py:438
  121.3 2.3 %copy.9 = bf16[2,1024,256]{2,1,0:T(8,128)(2,1)} copy(bf16[2,1024,256]{2,1,0:T(8,128)(2,1)} %shard_map.73) | data formatting | bytes 2097152

commit v2 on v1

--- a/solution.py
+++ b/solution.py
@@ -306,15 +306,29 @@
         for k in range(1, n_row):
             total = total + swr[h, k].astype(F32)
         swg[h, row] = total.astype(BF16)
-        for d in range(1, n_row):
-            g_copy(h, d, row).start()
-
-    def g_copy(h, d, slot):
+        for e in range(1, line):
+            g_along(h, e, row).start()
+        g_across(h, 0, row).start()
+
+    def g_along(h, e, slot):
         return pltpu.make_async_remote_copy(
             src_ref=swg.at[h, slot], dst_ref=swg.at[h, slot],
-            send_sem=g_send.at[h, d], recv_sem=g_recv.at[h, d],
-            device_id=(lax.rem(row + d, n_row), col), device_id_type=MESH,
-        )
+            send_sem=g_send.at[h, e], recv_sem=g_recv.at[h, slot],
+            device_id=(2 * lax.rem(z + e, line) + x, col), device_id_type=MESH,
+        )
+
+    def g_across(h, e, slot):
+        return pltpu.make_async_remote_copy(
+            src_ref=swg.at[h, slot], dst_ref=swg.at[h, slot],
+            send_sem=g_send.at[h, line + e], recv_sem=g_recv.at[h, slot],
+            device_id=(mate, col), device_id_type=MESH,
+        )
+
+    def relay_sweep(h):
+        for e in range(1, line):
+            slot = 2 * lax.rem(z + line - e, line) + x
+            g_along(h, e, slot).wait_recv()
+            g_across(h, e, slot).start()
 
     def add_received(h):
         for g in range(n_col - 1):
@@ -328,8 +342,8 @@
             acc[h, i] = total
 
     def finish(h):
-        for d in range(1, n_row):
-            g_copy(h, d, lax.rem(row + n_row - d, n_row)).wait_recv()
+        for e in range(line):
+            g_across(h, e, 2 * lax.rem(z + e, line) + 1 - x).wait_recv()
 
         @pl.loop(0, t_rows)
         def _(i):
@@ -367,6 +381,8 @@
     for h in range(subs):
         add_received(h)
     for h in range(subs):
+        relay_sweep(h)
+    for h in range(subs):
         finish(h)
 
     @pl.loop(0, steps)
@@ -407,8 +423,10 @@
         uv_copy(0, d, col).wait_send()
         uv_copy(1, d, col).wait_send()
     for h in range(subs):
-        for d in range(1, n_row):
-            g_copy(h, d, row).wait_send()
+        for e in range(line):
+            if e > 0:
+                g_along(h, e, row).wait_send()
+            g_across(h, e, row).wait_send()
 
 
 def shards(n_row, n_col, x_rhs, panel_u, panel_v, panel_rank, tile_p, tile_q, tile_rank):

time: 126 us -> 124 us (0.984); the launches traced: 124 us -> 123 us
  no operation moved by 1% of the time
where the time goes in v2:
time: 124 us; the launch traced here: 123 us
  Pallas kernels  121 us (98%)
  local copies, waits for them, and re-layouts  2.26 us (2%)
    pallas_call x1, Pallas kernels, shards(): pl.pallas_call(functools.partial(kernel, n_row, n_col), out_shape=jax.Sha...  121 us

profile of v2, /device:TPU:29, one launch (start us, length us, event | category | flops | bytes accessed | tf_op | source)
XLA Modules:
  0.0 123.2 jit_solution(13228639044755054573)
XLA Ops:
  0.0 120.9 %shard_map.73 = bf16[2,1024,256]{2,1,0:T(8,128)(2,1)} custom-call(s32[2,4]{1,0:T(2,128)} %tile_rank.1, s32[16]{0:T(128)} %panel_rank.1, bf16[4,128,1024]{2,1,0:T(8,128)(2,1)} %x_in.1, bf16[2,256,256]{2,1,0:T(8,128)(2,1)} %u_in.1, bf16[2,256,256]{2,1,0:T(8,128)(2,1)} %v_in.1, bf16[2,4,1024,256]{3,2,1,0:T(8,128)(2,1)} %p_in.1, bf16[2,4,1024,256]{3,2,1,0:T(8,128)(2,1)} %q_in.1), custom_call_target="tpu_custom_call" | custom-call | flops 10737418240 | bytes 20971520 | tf_op jit(solution)/shard_map/pallas_call | solution.py:456
  120.9 2.3 %copy.9 = bf16[2,1024,256]{2,1,0:T(8,128)(2,1)} copy(bf16[2,1024,256]{2,1,0:T(8,128)(2,1)} %shard_map.73) | data formatting | bytes 2097152

commit v3 on v2

--- a/solution.py
+++ b/solution.py
@@ -74,7 +74,7 @@
     subs = swr.shape[0]
     steps = n_col * subs
     away = steps - subs
-    ahead = 2
+    ahead = 2 * subs
     half = t_cols // 2
     line = n_row // 2
     row = lax.axis_index("row")
@@ -240,57 +240,65 @@
             device_id=(k, owner(s)), device_id_type=MESH,
         )
 
-    def compute(s):
-        low_copy(s, twin + 1 - 2 * x).wait_recv()
-        high_copy(s, twin + 1 - 2 * x).wait_recv()
-        for e in range(1, line // 2):
-            pair = lax.rem(z // 2 + e, line // 2)
-            for b in range(2):
-                x_copy(s, 2 * (2 * pair + b) + 1 - x, ACROSS).wait_recv()
+    def compute(span, own):
+        wide = len(span) * width
+
+        def block(j):
+            parts = [xg[s, :, j].reshape(order, width) for s in span]
+            return parts[0] if len(parts) == 1 else jnp.concatenate(parts, axis=1)
+
+        for s in span:
+            low_copy(s, twin + 1 - 2 * x).wait_recv()
+            high_copy(s, twin + 1 - 2 * x).wait_recv()
+            for e in range(1, line // 2):
+                pair = lax.rem(z // 2 + e, line // 2)
+                for b in range(2):
+                    x_copy(s, 2 * (2 * pair + b) + 1 - x, ACROSS).wait_recv()
 
         @pl.when(inside)
         def _():
             for i in range(t_rows):
-                block = xg[s, :, first + i].reshape(order, width)
-                proj = dot(ut[i], block).astype(BF16)
+                proj = dot(ut[i], block(first + i)).astype(BF16)
                 term = dot(vg[:, i].reshape(order, rank_cap), proj)
                 if i == 0:
-                    sweep_acc[...] = term
+                    sweep_acc[:, :wide] = term
                 else:
-                    sweep_acc[...] += term
-            swb[s] = sweep_acc[...].astype(BF16).reshape(n_row, x_rows, width)
-
-            @pl.loop(0, n_row)
-            def _(k):
-                mine = jnp.logical_and(k == row, s >= away)
-
-                @pl.when(mine)
-                def _():
-                    swr[s - away, row] = swb[s, row]
-
-                @pl.when(jnp.logical_not(mine))
-                def _():
-                    sw_copy(s, k).start()
+                    sweep_acc[:, :wide] += term
+            for n, s in enumerate(span):
+                cut = sweep_acc[:, n * width : (n + 1) * width]
+                swb[s] = cut.astype(BF16).reshape(n_row, x_rows, width)
+
+                @pl.loop(0, n_row)
+                def _(k):
+                    if own:
+                        @pl.when(k == row)
+                        def _():
+                            swr[s - away, row] = swb[s, row]
+
+                        @pl.when(k != row)
+                        def _():
+                            sw_copy(s, k).start()
+                    else:
+                        sw_copy(s, k).start()
 
         @pl.loop(0, t_rows)
         def _(i):
             total = None
             for j in range(t_cols):
-                proj = dot(qt[i, j], xg[s, :, j].reshape(order, width)).astype(BF16)
+                proj = dot(qt[i, j], block(j)).astype(BF16)
                 term = dot(pv[i, j], proj)
                 total = term if total is None else total + term
 
-            @pl.when(s < away)
-            def _():
-                sbuf[s, i] = total.astype(BF16)
-
-            @pl.when(s >= away)
-            def _():
-                acc[lax.rem(s, subs), i] = total
-
-        @pl.when(s < away)
-        def _():
-            b_copy(s).start()
+            for n, s in enumerate(span):
+                cut = total[:, n * width : (n + 1) * width]
+                if own:
+                    acc[s - away, i] = cut
+                else:
+                    sbuf[s, i] = cut.astype(BF16)
+
+        if not own:
+            for s in span:
+                b_copy(s).start()
 
     def reduce_sweep(h):
         for k in range(n_row):
@@ -373,9 +381,13 @@
             for d in range(2, line):
                 forward(s, d)
 
-        @pl.when(s > 0)
-        def _():
-            compute(s - 1)
+        @pl.when(jnp.logical_and(jnp.logical_and(s > 0, s <= away), lax.rem(s, subs) == 0))
+        def _():
+            compute([s - subs + h for h in range(subs)], False)
+
+        @pl.when(s > away)
+        def _():
+            compute([s - 1], True)
 
     reduce_sweep(subs - 1)
     for h in range(subs):
@@ -434,7 +446,7 @@
     x_rows, n_rhs = x_rhs.shape[1:]
     u_rows = panel_u.shape[1]
     width = n_rhs // n_col
-    subs = 1
+    subs = 2
     part = width // subs
     steps = n_col * subs
     away = steps - subs
@@ -469,7 +481,7 @@
             pltpu.VMEM((t_rows, rank_cap, order), BF16),
             pltpu.VMEM((t_rows, rank_cap, order), BF16),
             pltpu.VMEM((subs, t_rows, order, part), F32),
-            pltpu.VMEM((order, part), F32),
+            pltpu.VMEM((order, width), F32),
             pltpu.VMEM((away, t_rows, order, part), BF16),
             pltpu.VMEM((away, t_rows, order, part), BF16),
             pltpu.VMEM((steps, n_row, x_rows, part), BF16),

time: 124 us -> 126 us (1.016)
  the two profiles are of different devices: /device:TPU:29 before, /device:TPU:1 now
where the time goes in v3:
time: 126 us
  Pallas kernels  124 us (98%)
  local copies, waits for them, and re-layouts  2.26 us (2%)
    pallas_call x1, Pallas kernels, shards(): pl.pallas_call(functools.partial(kernel, n_row, n_col), out_shape=jax.Sha...  124 us

profile of v3, /device:TPU:1, one launch (start us, length us, event | category | flops | bytes accessed | tf_op | source)
XLA Modules:
  0.0 125.9 jit_solution(17359626611743523369)
XLA Ops:
  0.0 123.7 %shard_map.73 = bf16[2,1024,256]{2,1,0:T(8,128)(2,1)} custom-call(s32[2,4]{1,0:T(2,128)} %tile_rank.1, s32[16]{0:T(128)} %panel_rank.1, bf16[4,128,1024]{2,1,0:T(8,128)(2,1)} %x_in.1, bf16[2,256,256]{2,1,0:T(8,128)(2,1)} %u_in.1, bf16[2,256,256]{2,1,0:T(8,128)(2,1)} %v_in.1, bf16[2,4,1024,256]{3,2,1,0:T(8,128)(2,1)} %p_in.1, bf16[2,4,1024,256]{3,2,1,0:T(8,128)(2,1)} %q_in.1), custom_call_target="tpu_custom_call" | custom-call | flops 10737418240 | bytes 20971520 | tf_op jit(solution)/shard_map/pallas_call | solution.py:468
  123.7 2.3 %copy.9 = bf16[2,1024,256]{2,1,0:T(8,128)(2,1)} copy(bf16[2,1024,256]{2,1,0:T(8,128)(2,1)} %shard_map.73) | data formatting | bytes 2097152

commit v4 on v2

--- a/solution.py
+++ b/solution.py
@@ -240,7 +240,7 @@
             device_id=(k, owner(s)), device_id_type=MESH,
         )
 
-    def compute(s):
+    def sweep_terms(s):
         low_copy(s, twin + 1 - 2 * x).wait_recv()
         high_copy(s, twin + 1 - 2 * x).wait_recv()
         for e in range(1, line // 2):
@@ -272,7 +272,8 @@
                 def _():
                     sw_copy(s, k).start()
 
-        @pl.loop(0, t_rows)
+    def base_rows(s, lo, hi):
+        @pl.loop(lo, hi)
         def _(i):
             total = None
             for j in range(t_cols):
@@ -288,8 +289,7 @@
             def _():
                 acc[lax.rem(s, subs), i] = total
 
-        @pl.when(s < away)
-        def _():
+        if lo == 0 and hi == t_rows:
             b_copy(s).start()
 
     def reduce_sweep(h):
@@ -351,7 +351,7 @@
             late = dot(ug[:, i].reshape(order, rank_cap), back)
             out[i, :, h * width : (h + 1) * width] = (acc[h, i] - late).astype(BF16)
 
-    @pl.loop(0, steps + 1)
+    @pl.loop(0, steps)
     def _(s):
         @pl.when(s < steps)
         def _():
@@ -363,11 +363,6 @@
         def _():
             own_sends(s + ahead)
 
-        @pl.when(s == steps)
-        def _():
-            for h in range(subs - 1):
-                reduce_sweep(h)
-
         @pl.when(s < steps)
         def _():
             for d in range(2, line):
@@ -375,14 +370,18 @@
 
         @pl.when(s > 0)
         def _():
-            compute(s - 1)
-
-    reduce_sweep(subs - 1)
-    for h in range(subs):
-        add_received(h)
+            sweep_terms(s - 1)
+            base_rows(s - 1, 0, t_rows)
+
+    last = jnp.int32(steps - 1)
+    sweep_terms(last)
+    base_rows(last, 0, t_rows // 2)
+    reduce_sweep(0)
+    base_rows(last, t_rows // 2, t_rows)
     for h in range(subs):
         relay_sweep(h)
     for h in range(subs):
+        add_received(h)
         finish(h)
 
     @pl.loop(0, steps)
@@ -446,6 +445,7 @@
         and n_row % 4 == 0
         and n_col > 1
         and n_col & (n_col - 1) == 0
+        and t_rows > 1
         and t_cols % t_rows == 0
         and t_cols % 2 == 0
     )

time: 124 us -> 124 us (level)
  no operation moved by 1% of the time
where the time goes in v4:
time: 124 us; the launch traced here: 123 us
  Pallas kernels  121 us (98%)
  local copies, waits for them, and re-layouts  2.26 us (2%)
    pallas_call x1, Pallas kernels, shards(): pl.pallas_call(functools.partial(kernel, n_row, n_col), out_shape=jax.Sha...  121 us

profile of v4, /device:TPU:29, one launch (start us, length us, event | category | flops | bytes accessed | tf_op | source)
XLA Modules:
  0.0 123.0 jit_solution(9027103897413204629)
XLA Ops:
  0.0 120.7 %shard_map.73 = bf16[2,1024,256]{2,1,0:T(8,128)(2,1)} custom-call(s32[2,4]{1,0:T(2,128)} %tile_rank.1, s32[16]{0:T(128)} %panel_rank.1, bf16[4,128,1024]{2,1,0:T(8,128)(2,1)} %x_in.1, bf16[2,256,256]{2,1,0:T(8,128)(2,1)} %u_in.1, bf16[2,256,256]{2,1,0:T(8,128)(2,1)} %v_in.1, bf16[2,4,1024,256]{3,2,1,0:T(8,128)(2,1)} %p_in.1, bf16[2,4,1024,256]{3,2,1,0:T(8,128)(2,1)} %q_in.1), custom_call_target="tpu_custom_call" | custom-call | flops 10737418240 | bytes 20971520 | tf_op jit(solution)/shard_map/pallas_call | solution.py:456
  120.7 2.3 %copy.9 = bf16[2,1024,256]{2,1,0:T(8,128)(2,1)} copy(bf16[2,1024,256]{2,1,0:T(8,128)(2,1)} %shard_map.73) | data formatting | bytes 2097152
